TPU v7x, 32 devices: a whole 2x2x4 slice. The times are simulated.
32 devices in a mesh: lat: 4 (over x, core), lon: 8 (over z, y).
Axes of the slice: x: 2, y: 2, z: 4, core: 2. Of those that a mesh axis runs over, the one named last changes fastest.
Arguments:
- queries: bfloat16 [64, 128, 1536], P('lat', 'lon'), may hold values from -12 to 12
- key_tokens: bfloat16 [64, 128, 1536], P('lat', 'lon'), may hold values from -4 to 4
- value_tokens: bfloat16 [64, 128, 1536], P('lat', 'lon'), may hold values from -6 to 6
- block_lists: int32 [8, 8, 8], P('lat', 'lon'), may hold values from 0 to 9, as said below
- band_rows: int32 [4, 128], P('lat', 'lon'), may hold values from 0 to 255, as said below
Outputs:
- attended: bfloat16 [64, 128, 1536], P('lat', 'lon')
Inputs may be any that keep to these rules, and one draw needn't show every extreme that they name: `block_lists`: entry 0 of the list of query block b of a tile is its own block, 4 + b; the other entries are distinct candidate numbers, also distinct from entry 0. `band_rows`: the 16 token numbers of each tile are distinct.
All inputs are finite; a program needn't handle non-finite values.
Results may differ from a plain program's by a relative error of at most 0.0047.
Values may be sent and summed in bfloat16 or wider, within the bound.
A program may use at most 128 MiB of HBM per device.

v0:
```python
import jax
import jax.numpy as jnp
from jax import lax
from jax.sharding import PartitionSpec as P

H = 24
HD = 64
BR = 8
BW = 16


def from_behind(value, axis, steps):
    count = lax.axis_size(axis)
    pairs = [(source, (source + steps) % count) for source in range(count)]
    return lax.ppermute(value, axis, pairs)


def block_attention(q_rows, key_set, value_set, live_mask):
    count = q_rows.shape[0]
    q_heads = q_rows.reshape(count, H, HD)
    k_heads = key_set.reshape(key_set.shape[0], H, HD)
    v_heads = value_set.reshape(value_set.shape[0], H, HD)
    scores = jnp.einsum(
        "qhd,khd->hqk", q_heads, k_heads, preferred_element_type=jnp.float32
    ) * HD ** (-0.5)
    scores = jnp.where(live_mask[None, None, :], scores, -jnp.inf)
    row_max = jnp.max(scores, axis=-1, keepdims=True)
    exp_scores = jnp.exp(scores - row_max)
    totals = jnp.sum(exp_scores, axis=-1)
    weights = exp_scores.astype(jnp.bfloat16)
    mixture = jnp.einsum("hqk,khd->qhd", weights, v_heads, preferred_element_type=jnp.float32)
    mixture = mixture / jnp.transpose(totals)[:, :, None]
    return mixture.reshape(count, H * HD).astype(jnp.bfloat16)


def local(queries, key_tokens, value_tokens, block_lists, band_rows):
    tile_lat, tile_lon, feature = queries.shape
    block_len = BR * BW
    tile_blocks = tile_lat // BR
    lat_size = lax.axis_size("lat")
    west_two = from_behind((key_tokens, value_tokens), "lon", 2)
    west_one = from_behind((key_tokens, value_tokens), "lon", 1)
    east_one = from_behind((key_tokens, value_tokens), "lon", -1)
    east_two = from_behind((key_tokens, value_tokens), "lon", -2)
    sources = (west_two, west_one, (key_tokens, value_tokens), east_one, east_two)
    cand_keys = jnp.concatenate(
        [entry[0].reshape(tile_blocks, block_len, feature) for entry in sources], 0
    )
    cand_values = jnp.concatenate(
        [entry[1].reshape(tile_blocks, block_len, feature) for entry in sources], 0
    )
    picked_keys = key_tokens.reshape(tile_lat * tile_lon, feature)[band_rows[0]]
    picked_values = value_tokens.reshape(tile_lat * tile_lon, feature)[band_rows[0]]
    band_keys, band_values = (
        lax.all_gather(picked_keys, "lon", axis=0, tiled=True),
        lax.all_gather(picked_values, "lon", axis=0, tiled=True),
    )
    lat_at = lax.axis_index("lat")
    is_polar = (lat_at == 0) | (lat_at == lat_size - 1)
    listed_all = block_lists[:, 0, :]
    band_live = jnp.ones((band_keys.shape[0],), jnp.bool_)
    query_blocks = queries.reshape(tile_blocks, block_len, feature)

    def one_block(inputs):
        q_rows, listed = inputs
        near_keys = cand_keys[listed].reshape(-1, feature)
        near_values = cand_values[listed].reshape(-1, feature)
        near_live = jnp.ones((near_keys.shape[0],), jnp.bool_)

        def with_band():
            key_set = jnp.concatenate([near_keys, band_keys], 0)
            value_set = jnp.concatenate([near_values, band_values], 0)
            live_mask = jnp.concatenate([near_live, band_live], 0)
            return block_attention(q_rows, key_set, value_set, live_mask)

        def near_only():
            return block_attention(q_rows, near_keys, near_values, near_live)

        return lax.cond(is_polar, with_band, near_only)

    results = lax.map(one_block, (query_blocks, listed_all))
    return results.reshape(tile_lat, tile_lon, feature)


def solution(mesh):
    return jax.shard_map(
        local,
        mesh=mesh,
        in_specs=(
            P("lat", "lon", None),
            P("lat", "lon", None),
            P("lat", "lon", None),
            P("lat", "lon", None),
            P("lat", "lon"),
        ),
        out_specs=P("lat", "lon", None),
        check_vma=False,
    )
```

profile of v0, /device:TPU:0, one launch (start us, length us, event | category | flops | bytes accessed | tf_op | source)
XLA Modules:
  0.0 260.5 jit_solution(4554898593392633813)
XLA Ops:
  3.0 3.2 %collective-permute-start.2 = (bf16[16,16,1536]{2,1,0:T(8,128)(2,1)}, bf16[16,16,1536]{2,1,0:T(8,128)(2,1)S(1)}, u32[]{:S(2)}, u32[]{:S(2)}) collective-permute-start(bf16[16,16,1536]{2,1,0:T(8,128)(2,1)} %param.10), channel_id=1, source_target_pairs={{0,7},{1,0},{2,1},{3,2},{4,3},{5,4},{6,5},{7,6},{8,15},{9,8},{10,9... | collective-permute-start | bytes 2359304 | tf_op jit(solution)/shard_map/ppermute | solution.py:15
  14.7 84.6 %all-gather = bf16[128,1536]{1,0:T(8,128)(2,1)S(1)} all-gather(bf16[16,1536]{1,0:T(8,128)(2,1)} %gather_fusion.2), channel_id=2, replica_groups=mesh['lat'=4,'lon'=8] {'lon'}, dimensions={0}, use_global_device_ids=true | all-gather | bytes 442368 | tf_op jit(solution)/shard_map/all_gather | solution.py:56
  100.2 37.7 %all-gather.1 = bf16[128,1536]{1,0:T(8,128)(2,1)S(1)} all-gather(bf16[16,1536]{1,0:T(8,128)(2,1)} %gather_fusion.3), channel_id=3, replica_groups=mesh['lat'=4,'lon'=8] {'lon'}, dimensions={0}, use_global_device_ids=true | all-gather | bytes 442368 | tf_op jit(solution)/shard_map/all_gather | solution.py:55
  140.0 6.4 %collective-permute-start.7 = (bf16[16,16,1536]{2,1,0:T(8,128)(2,1)S(1)}, bf16[16,16,1536]{2,1,0:T(8,128)(2,1)S(1)}, u32[]{:S(2)}, u32[]{:S(2)}) collective-permute-start(bf16[16,16,1536]{2,1,0:T(8,128)(2,1)S(1)} %copy-done.5), channel_id=1, source_target_pairs={{0,6},{1,7},{2,0},{3,1},{4,2},{5,3},{6,4},{7,5},{8,14},{9,15},{10,... | collective-permute-start | bytes 2359304 | tf_op jit(solution)/shard_map/ppermute | solution.py:15
  149.0 7.0 %collective-permute-done.6 = bf16[16,16,1536]{2,1,0:T(8,128)(2,1)S(1)} collective-permute-done((bf16[16,16,1536]{2,1,0:T(8,128)(2,1)}, bf16[16,16,1536]{2,1,0:T(8,128)(2,1)S(1)}, u32[]{:S(2)}, u32[]{:S(2)}) %collective-permute-start.6) | collective-permute-done | bytes 786464 | tf_op jit(solution)/shard_map/ppermute | solution.py:15
  156.0 8.3 %collective-permute-done.7 = bf16[16,16,1536]{2,1,0:T(8,128)(2,1)S(1)} collective-permute-done((bf16[16,16,1536]{2,1,0:T(8,128)(2,1)S(1)}, bf16[16,16,1536]{2,1,0:T(8,128)(2,1)S(1)}, u32[]{:S(2)}, u32[]{:S(2)}) %collective-permute-start.7) | collective-permute-done | bytes 786464 | tf_op jit(solution)/shard_map/ppermute | solution.py:15
  164.6 8.1 %collective-permute-done.3 = bf16[16,16,1536]{2,1,0:T(8,128)(2,1)S(1)} collective-permute-done((bf16[16,16,1536]{2,1,0:T(8,128)(2,1)S(1)}, bf16[16,16,1536]{2,1,0:T(8,128)(2,1)S(1)}, u32[]{:S(2)}, u32[]{:S(2)}) %collective-permute-start.3) | collective-permute-done | bytes 786464 | tf_op jit(solution)/shard_map/ppermute | solution.py:15
  174.7 85.8 %while.10 = (s32[]{:T(128)}, bf16[2,128,1536]{2,1,0:T(8,128)(2,1)}, pred[]{:T(512)}, bf16[2,128,1536]{2,1,0:T(8,128)(2,1)}, s32[2,8]{1,0:T(2,128)S(1)}, /*index=...) while((s32[]{:T(128)}, bf16[2,128,1536]{2,1,0:T(8,128)(2,1)}, ...), condition=%wide.region_7.8_spmd, body=%wide.region_0.7_spmd.sunk | while | flops 948825088 | bytes 161284544 | solution.py:81
  178.8 4.6 %gather_fusion = bf16[8,128,1536]{2,1,0:T(8,128)(2,1)} fusion(bf16[10,128,1536]{2,1,0:T(8,128)(2,1)} %get-tuple-element.216, s32[1024]{0:T(1024)S(1)} %pad_clamp_fusion.3), kind=kCustom, calls=%fused_computation.clone.1 | custom fusion | bytes 6291488 | tf_op jit(solution)/shard_map/while/body/eval_jaxpr/gather | solution.py:66
  183.4 32.3 %conditional.7 = (bf16[1,128,1536]{1,2,0:T(8,128)(2,1)}) conditional(s32[]{:T(128)} %convert_element_type.36, (bf16[128,1536]{0,1:T(8,128)(2,1)S(1)}, bf16[8,128,1536]{2,1,0:T(8,128)(2,1)}, bf16[8,128,1536]{2,1,0:T(8,128)(2,1)S(1)}) %tuple.49, (bf16[8,128,1536]{2,1,0:T(8,128)(2,1)S(1)}, bf16[128,1536]{0,1:T(8,128)(2,1)}, ...), branch_computations={%region_1.3_spmd, %region_4.6_spmd} | conditional | flops 948824064 | bytes 145551456
  183.4 5.0 %copy.14 = bf16[8,128,1536]{1,0,2:T(8,128)(2,1)} copy(bf16[8,128,1536]{2,1,0:T(8,128)(2,1)} %get-tuple-element.102) | data formatting | bytes 6291456 | tf_op jit(solution)/shard_map
  188.4 5.8 %concatenate.17 = bf16[1024,24,64]{0,2,1:T(8,128)(2,1)} reshape(bf16[8,128,1536]{1,0,2:T(8,128)(2,1)} %copy.14) | data formatting | bytes 6291456 | tf_op jit(solution)/shard_map/while/body/eval_jaxpr/cond/branch_1_fun/concatenate | solution.py:71
  194.2 3.5 %copy.13 = bf16[8,128,1536]{1,0,2:T(8,128)(2,1)} copy(bf16[8,128,1536]{2,1,0:T(8,128)(2,1)S(1)} %get-tuple-element.100) | data formatting | bytes 6291456 | tf_op jit(solution)/shard_map
  197.7 5.8 %concatenate.2 = bf16[1024,24,64]{0,2,1:T(8,128)(2,1)} reshape(bf16[8,128,1536]{1,0,2:T(8,128)(2,1)} %copy.13) | data formatting | bytes 6291456 | tf_op jit(solution)/shard_map/while/body/eval_jaxpr/cond/branch_1_fun/concatenate | solution.py:72
  203.4 4.4 %bitcast_reduce_fusion = (f32[24,128]{1,0:T(8,128)S(1)}, f32[24,1152,128]{2,1,0:T(8,128)S(1)}) fusion(bf16[128,24,64]{0,2,1:T(8,128)(2,1)S(1)} %bitcast.99, bf16[128,24,64]{0,2,1:T(8,128)(2,1)} %bitcast.100, bf16[1024,24,64]{0,2,1:T(8,128)(2,1)} %concatenate.17), kind=kOutput, calls=%fused_computation.15 | convolution fusion | flops 467137536 | bytes 18100224 | tf_op jit(solution)/shard_map/while/body/eval_jaxpr/cond/branch_1_fun/qhd,khd->hqk/dot_general | solution.py:23
  210.2 5.5 %fusion.32 = bf16[128,24,64]{0,2,1:T(8,128)(2,1)} fusion(f32[24,1152,128]{2,1,0:T(8,128)S(1)} %get-tuple-element.135, f32[24,128]{1,0:T(8,128)S(1)} %get-tuple-element.134, bf16[128,24,64]{0,2,1:T(8,128)(2,1)S(1)} %bitcast.110, bf16[1024,24,64]{0,2,1:T(8,128)(2,1)} %concatenate.2, f32[128,24]{0,1:T(8,128)S(1)} %bitcast.112), kind=kOutput, calls=%fused_computation.30 | convolution fusion | flops 471072768 | bytes 18112512 | tf_op jit(solution)/shard_map/while/body/eval_jaxpr/cond/branch_1_fun/hqk,khd->qhd/dot_general | solution.py:31
  221.7 4.6 %gather_fusion = bf16[8,128,1536]{2,1,0:T(8,128)(2,1)} fusion(bf16[10,128,1536]{2,1,0:T(8,128)(2,1)} %get-tuple-element.216, s32[1024]{0:T(1024)S(1)} %pad_clamp_fusion.3), kind=kCustom, calls=%fused_computation.clone.1 | custom fusion | bytes 6291488 | tf_op jit(solution)/shard_map/while/body/eval_jaxpr/gather | solution.py:66
  226.3 32.3 %conditional.7 = (bf16[1,128,1536]{1,2,0:T(8,128)(2,1)}) conditional(s32[]{:T(128)} %convert_element_type.36, (bf16[128,1536]{0,1:T(8,128)(2,1)S(1)}, bf16[8,128,1536]{2,1,0:T(8,128)(2,1)}, bf16[8,128,1536]{2,1,0:T(8,128)(2,1)S(1)}) %tuple.49, (bf16[8,128,1536]{2,1,0:T(8,128)(2,1)S(1)}, bf16[128,1536]{0,1:T(8,128)(2,1)}, ...), branch_computations={%region_1.3_spmd, %region_4.6_spmd} | conditional | flops 948824064 | bytes 145551456
  226.3 5.0 %copy.14 = bf16[8,128,1536]{1,0,2:T(8,128)(2,1)} copy(bf16[8,128,1536]{2,1,0:T(8,128)(2,1)} %get-tuple-element.102) | data formatting | bytes 6291456 | tf_op jit(solution)/shard_map
  231.3 5.8 %concatenate.17 = bf16[1024,24,64]{0,2,1:T(8,128)(2,1)} reshape(bf16[8,128,1536]{1,0,2:T(8,128)(2,1)} %copy.14) | data formatting | bytes 6291456 | tf_op jit(solution)/shard_map/while/body/eval_jaxpr/cond/branch_1_fun/concatenate | solution.py:71
  237.1 3.5 %copy.13 = bf16[8,128,1536]{1,0,2:T(8,128)(2,1)} copy(bf16[8,128,1536]{2,1,0:T(8,128)(2,1)S(1)} %get-tuple-element.100) | data formatting | bytes 6291456 | tf_op jit(solution)/shard_map
  240.6 5.8 %concatenate.2 = bf16[1024,24,64]{0,2,1:T(8,128)(2,1)} reshape(bf16[8,128,1536]{1,0,2:T(8,128)(2,1)} %copy.13) | data formatting | bytes 6291456 | tf_op jit(solution)/shard_map/while/body/eval_jaxpr/cond/branch_1_fun/concatenate | solution.py:72
  246.4 4.4 %bitcast_reduce_fusion = (f32[24,128]{1,0:T(8,128)S(1)}, f32[24,1152,128]{2,1,0:T(8,128)S(1)}) fusion(bf16[128,24,64]{0,2,1:T(8,128)(2,1)S(1)} %bitcast.99, bf16[128,24,64]{0,2,1:T(8,128)(2,1)} %bitcast.100, bf16[1024,24,64]{0,2,1:T(8,128)(2,1)} %concatenate.17), kind=kOutput, calls=%fused_computation.15 | convolution fusion | flops 467137536 | bytes 18100224 | tf_op jit(solution)/shard_map/while/body/eval_jaxpr/cond/branch_1_fun/qhd,khd->hqk/dot_general | solution.py:23
  253.1 5.5 %fusion.32 = bf16[128,24,64]{0,2,1:T(8,128)(2,1)} fusion(f32[24,1152,128]{2,1,0:T(8,128)S(1)} %get-tuple-element.135, f32[24,128]{1,0:T(8,128)S(1)} %get-tuple-element.134, bf16[128,24,64]{0,2,1:T(8,128)(2,1)S(1)} %bitcast.110, bf16[1024,24,64]{0,2,1:T(8,128)(2,1)} %concatenate.2, f32[128,24]{0,1:T(8,128)S(1)} %bitcast.112), kind=kOutput, calls=%fused_computation.30 | convolution fusion | flops 471072768 | bytes 18112512 | tf_op jit(solution)/shard_map/while/body/eval_jaxpr/cond/branch_1_fun/hqk,khd->qhd/dot_general | solution.py:31
  (58 shorter events, 36.0 us)
Async XLA Ops:
  0.0 140.0 %copy-start.5 = (bf16[16,16,1536]{2,1,0:T(8,128)(2,1)S(1)}, bf16[16,16,1536]{2,1,0:T(8,128)(2,1)}, u32[]{:S(2)}) copy-start(bf16[16,16,1536]{2,1,0:T(8,128)(2,1)} %param.11) | copy-start | bytes 2359300
  0.0 147.6 %copy-start.6 = (bf16[16,16,1536]{2,1,0:T(8,128)(2,1)S(1)}, bf16[16,16,1536]{2,1,0:T(8,128)(2,1)}, u32[]{:S(2)}) copy-start(bf16[16,16,1536]{2,1,0:T(8,128)(2,1)} %param.10) | copy-start | bytes 2359300
  0.0 138.8 %collective-permute-start.4 = (bf16[16,16,1536]{2,1,0:T(8,128)(2,1)}, bf16[16,16,1536]{2,1,0:T(8,128)(2,1)}, u32[]{:S(2)}, u32[]{:S(2)}) collective-permute-start(bf16[16,16,1536]{2,1,0:T(8,128)(2,1)} %param.11), channel_id=1, source_target_pairs={{0,2},{1,3},{2,4},{3,5},{4,6},{5,7},{6,0},{7,1},{8,10},{9,11},{10,... | collective-permute-start | bytes 2359304 | tf_op jit(solution)/shard_map/ppermute | solution.py:15
  3.0 161.5 %collective-permute-start.2 = (bf16[16,16,1536]{2,1,0:T(8,128)(2,1)}, bf16[16,16,1536]{2,1,0:T(8,128)(2,1)S(1)}, u32[]{:S(2)}, u32[]{:S(2)}) collective-permute-start(bf16[16,16,1536]{2,1,0:T(8,128)(2,1)} %param.10), channel_id=1, source_target_pairs={{0,7},{1,0},{2,1},{3,2},{4,3},{5,4},{6,5},{7,6},{8,15},{9,8},{10,9... | collective-permute-start | bytes 2359304 | tf_op jit(solution)/shard_map/ppermute | solution.py:15
  6.2 158.1 %collective-permute-start.1 = (bf16[16,16,1536]{2,1,0:T(8,128)(2,1)}, bf16[16,16,1536]{2,1,0:T(8,128)(2,1)S(1)}, u32[]{:S(2)}, u32[]{:S(2)}) collective-permute-start(bf16[16,16,1536]{2,1,0:T(8,128)(2,1)} %param.10), channel_id=1, source_target_pairs={{0,1},{1,2},{2,3},{3,4},{4,5},{5,6},{6,7},{7,0},{8,9},{9,10},{10,1... | collective-permute-start | bytes 2359304 | tf_op jit(solution)/shard_map/ppermute | solution.py:15
  6.2 133.8 %collective-permute-start = (bf16[16,16,1536]{2,1,0:T(8,128)(2,1)}, bf16[16,16,1536]{2,1,0:T(8,128)(2,1)}, u32[]{:S(2)}, u32[]{:S(2)}) collective-permute-start(bf16[16,16,1536]{2,1,0:T(8,128)(2,1)} %param.10), channel_id=1, source_target_pairs={{0,2},{1,3},{2,4},{3,5},{4,6},{5,7},{6,0},{7,1},{8,10},{9,11},{10,... | collective-permute-start | bytes 2359304 | tf_op jit(solution)/shard_map/ppermute | solution.py:15
  6.6 141.0 %collective-permute-start.5 = (bf16[16,16,1536]{2,1,0:T(8,128)(2,1)}, bf16[16,16,1536]{2,1,0:T(8,128)(2,1)}, u32[]{:S(2)}, u32[]{:S(2)}) collective-permute-start(bf16[16,16,1536]{2,1,0:T(8,128)(2,1)} %param.11), channel_id=1, source_target_pairs={{0,1},{1,2},{2,3},{3,4},{4,5},{5,6},{6,7},{7,0},{8,9},{9,10},{10,1... | collective-permute-start | bytes 2359304 | tf_op jit(solution)/shard_map/ppermute | solution.py:15
  138.8 17.2 %collective-permute-start.6 = (bf16[16,16,1536]{2,1,0:T(8,128)(2,1)}, bf16[16,16,1536]{2,1,0:T(8,128)(2,1)S(1)}, u32[]{:S(2)}, u32[]{:S(2)}) collective-permute-start(bf16[16,16,1536]{2,1,0:T(8,128)(2,1)} %param.11), channel_id=1, source_target_pairs={{0,7},{1,0},{2,1},{3,2},{4,3},{5,4},{6,5},{7,6},{8,15},{9,8},{10,9... | collective-permute-start | bytes 2359304 | tf_op jit(solution)/shard_map/ppermute | solution.py:15
  140.0 24.3 %collective-permute-start.7 = (bf16[16,16,1536]{2,1,0:T(8,128)(2,1)S(1)}, bf16[16,16,1536]{2,1,0:T(8,128)(2,1)S(1)}, u32[]{:S(2)}, u32[]{:S(2)}) collective-permute-start(bf16[16,16,1536]{2,1,0:T(8,128)(2,1)S(1)} %copy-done.5), channel_id=1, source_target_pairs={{0,6},{1,7},{2,0},{3,1},{4,2},{5,3},{6,4},{7,5},{8,14},{9,15},{10,... | collective-permute-start | bytes 2359304 | tf_op jit(solution)/shard_map/ppermute | solution.py:15
  147.6 25.1 %collective-permute-start.3 = (bf16[16,16,1536]{2,1,0:T(8,128)(2,1)S(1)}, bf16[16,16,1536]{2,1,0:T(8,128)(2,1)S(1)}, u32[]{:S(2)}, u32[]{:S(2)}) collective-permute-start(bf16[16,16,1536]{2,1,0:T(8,128)(2,1)S(1)} %copy-done.6), channel_id=1, source_target_pairs={{0,6},{1,7},{2,0},{3,1},{4,2},{5,3},{6,4},{7,5},{8,14},{9,15},{10,... | collective-permute-start | bytes 2359304 | tf_op jit(solution)/shard_map/ppermute | solution.py:15
  164.3 10.4 %copy-start.8 = (s32[2,1,8]{2,1,0:T(1,128)S(1)}, s32[2,1,8]{2,1,0:T(1,128)}, u32[]{:S(2)}) copy-start(s32[2,1,8]{2,1,0:T(1,128)} %param.12) | copy-start | bytes 196
  164.4 8.4 %copy-start.4 = (bf16[10,128,1536]{2,1,0:T(8,128)(2,1)}, bf16[10,128,1536]{2,1,0:T(8,128)(2,1)S(1)}, u32[]{:S(2)}) copy-start(bf16[10,128,1536]{2,1,0:T(8,128)(2,1)S(1)} %bitcast_dynamic-update-slice_fusion) | copy-start | bytes 11796484
  172.8 1.9 copy-start.3
  207.8 2.3 copy-start.7
  250.8 2.3 copy-start.7
where the time goes:
time: 262 us; the launch traced here: 261 us
  blocking collectives  122 us (47%)
  local copies, waits for them, and re-layouts  74 us (28%)
  waiting for transfers between devices  23.4 us (9%)
  matrix products  19.8 us (8%)
  starting transfers between devices  15.5 us (6%)
  other arithmetic  5.3 us (2%)
    all_gather x1, blocking collectives, local(): lax.all_gather(picked_values, 'lon', axis=0, tiled=True)  84.6 us
    all_gather x1, blocking collectives, local(): lax.all_gather(picked_keys, 'lon', axis=0, tiled=True)  37.7 us
    ppermute x8, waiting for transfers between devices, from_behind(): return lax.ppermute(value, axis, pairs)  23.4 us
    another operation x8, local copies, waits for them, and re-layouts  16.9 us
    ppermute x8, starting transfers between devices, from_behind(): return lax.ppermute(value, axis, pairs)  15.5 us
    concatenate x2, local copies, waits for them, and re-layouts, with_band(): key_set = jnp.concatenate([near_keys, band_keys], 0)  11.6 us
    concatenate x2, local copies, waits for them, and re-layouts, with_band(): value_set = jnp.concatenate([near_values, band_values], 0)  11.5 us
    dot_general x2, matrix products, block_attention(): jnp.einsum('hqk,khd->qhd', weights, v_heads, preferred_element_type=jnp.f...  11 us
  transfers between devices with their start and end apart: 8, of which 3 were waited for; matrix products, arithmetic and copies ran while one was open for 4% of the time, Pallas kernels for 0%

commit v1 on v0

v1 whole, which is shorter than its diff:
```python
import functools

import jax
import jax.numpy as jnp
from jax import lax
from jax.experimental import pallas as pl
from jax.experimental.pallas import tpu as pltpu
from jax.sharding import PartitionSpec as P

HD = 64
BR = 8
BW = 16
PAIR = 2 * HD
MASKED = -1e30
MESH = pl.DeviceIdType.MESH


def kernel(
    n, n_lat, tile, picks,
    q_ref, k_ref, v_ref, lists_ref, rows_ref,
    out_ref,
    kv, staged, bias, send_sem, recv_sem, band_send, band_recv,
):
    groups = kv.shape[0]
    near = 5 * tile
    full = near + n * picks
    block = tile // 2
    me = lax.axis_index("lon")
    lat = lax.axis_index("lat")
    polar = (lat == 0) | (lat == n_lat - 1)
    odd = lax.rem(me, 2)
    partner = me + 1 - 2 * odd
    east = lax.rem(me + 2, n)
    west = lax.rem(me + n - 2, n)

    barrier = pltpu.get_barrier_semaphore()

    def greet(step, carry):
        pl.semaphore_signal(
            barrier, inc=1, device_id={"lon": lax.rem(me + step, n)}, device_id_type=MESH
        )
        return carry

    lax.fori_loop(1, n, greet, 0)

    for g in range(groups):
        columns = slice(g * PAIR, (g + 1) * PAIR)
        kv[g, 0, 2 * tile:3 * tile, :] = k_ref[:, columns]
        kv[g, 1, 2 * tile:3 * tile, :] = v_ref[:, columns]

    candidate = lax.broadcasted_iota(jnp.int32, (1, full), 1) // block
    for b in range(2):
        listed = candidate >= 10
        for slot in range(lists_ref.shape[2]):
            listed = listed | (candidate == lists_ref[b, 0, slot])
        bias[b:b + 1, :] = jnp.where(listed, 0.0, MASKED)

    @pl.when(polar)
    def _():
        row = lax.broadcasted_iota(jnp.int32, (picks, tile), 0)
        token = lax.broadcasted_iota(jnp.int32, (picks, tile), 1)
        hot = jnp.zeros((picks, tile), jnp.float32)
        for i in range(picks):
            hot = jnp.where((row == i) & (token == rows_ref[0, i]), 1.0, hot)
        hot = hot.astype(jnp.bfloat16)
        for which, ref in enumerate((k_ref, v_ref)):
            picked = jnp.dot(hot, ref[...], preferred_element_type=jnp.float32).astype(jnp.bfloat16)
            for g in range(groups):
                staged[g, which] = picked[:, g * PAIR:(g + 1) * PAIR]

    pl.semaphore_wait(barrier, n - 1)

    def tile_rows(t):
        return pl.ds(pl.multiple_of(t * tile, tile), tile)

    def own_copy(kind, g):
        target, t = ((east, 0), (west, 4), (partner, 1 + 2 * odd))[kind]
        return pltpu.make_async_remote_copy(
            src_ref=kv.at[g, :, tile_rows(2)],
            dst_ref=kv.at[g, :, tile_rows(t)],
            send_sem=send_sem.at[kind, g],
            recv_sem=recv_sem.at[kind, g],
            device_id={"lon": target},
            device_id_type=MESH,
        )

    def relay_copy(g):
        return pltpu.make_async_remote_copy(
            src_ref=kv.at[g, :, tile_rows(4 - 4 * odd)],
            dst_ref=kv.at[g, :, tile_rows(3 - 2 * odd)],
            send_sem=send_sem.at[3, g],
            recv_sem=recv_sem.at[3, g],
            device_id={"lon": partner},
            device_id_type=MESH,
        )

    def band_rows_of(j):
        return pl.ds(pl.multiple_of(near + j * picks, picks), picks)

    def band_copy(step):
        return pltpu.make_async_remote_copy(
            src_ref=staged,
            dst_ref=kv.at[:, :, band_rows_of(me)],
            send_sem=band_send.at[step],
            recv_sem=band_recv.at[step],
            device_id={"lon": lax.rem(me + step, n)},
            device_id_type=MESH,
        )

    def band_arrival(step):
        return pltpu.make_async_remote_copy(
            src_ref=staged,
            dst_ref=kv.at[:, :, band_rows_of(lax.rem(me + n - step, n))],
            send_sem=band_send.at[step],
            recv_sem=band_recv.at[step],
            device_id={"lon": lax.rem(me + step, n)},
            device_id_type=MESH,
        )

    def arrival(kind, t, g):
        return pltpu.make_async_remote_copy(
            src_ref=kv.at[g, :, tile_rows(2)],
            dst_ref=kv.at[g, :, tile_rows(t)],
            send_sem=send_sem.at[0, g],
            recv_sem=recv_sem.at[kind, g],
            device_id={"lon": partner},
            device_id_type=MESH,
        )

    @pl.when(polar)
    def _():
        def send(step, carry):
            band_copy(step).start()
            return carry

        lax.fori_loop(1, n, send, 0)
        for g in range(groups):
            kv[g, :, band_rows_of(me), :] = staged[g]

    def send_own(g, carry):
        for kind in range(3):
            own_copy(kind, g).start()
        return carry

    lax.fori_loop(0, groups, send_own, 0)

    def relay(g):
        arrival(1 - odd, 4 - 4 * odd, g).wait_recv()
        relay_copy(g).start()

    def attend(g, rows):
        columns = pl.ds(pl.multiple_of(g * PAIR, PAIR), PAIR)
        q = q_ref[:, columns] * jnp.bfloat16(HD ** -0.5)
        keys = kv[g, 0, 0:rows, :]
        values = jnp.concatenate(
            [kv[g, 1, 0:rows, :], jnp.ones((rows, PAIR), jnp.bfloat16)], axis=1
        )
        first = lax.broadcasted_iota(jnp.int32, (tile, PAIR), 1) < HD
        results = []
        for head in range(2):
            mine = first if head == 0 else ~first
            q_head = jnp.where(mine, q, jnp.zeros_like(q))
            scores = lax.dot_general(
                q_head, keys, (((1,), (1,)), ((), ())), preferred_element_type=jnp.float32
            )
            scores = scores.reshape(2, block, rows) + bias[:, 0:rows][:, None, :]
            scores = scores.reshape(tile, rows)
            row_max = jnp.max(scores, axis=-1, keepdims=True)
            weights = jnp.exp(scores - row_max).astype(jnp.bfloat16)
            mixed = jnp.dot(weights, values, preferred_element_type=jnp.float32)
            results.append(mixed[:, :PAIR] / mixed[:, PAIR:])
        out_ref[:, columns] = jnp.where(first, results[0], results[1]).astype(out_ref.dtype)

    relay(0)

    def step(g, carry):
        @pl.when(g + 1 < groups)
        def _():
            relay(g + 1)

        arrival(odd, 4 * odd, g).wait_recv()
        arrival(2, 3 - 2 * odd, g).wait_recv()
        arrival(3, 1 + 2 * odd, g).wait_recv()

        @pl.when(polar)
        def _():
            @pl.when(g == 0)
            def _():
                def take(s, c):
                    band_arrival(s).wait_recv()
                    return c

                lax.fori_loop(1, n, take, 0)

            attend(g, full)

        @pl.when(jnp.logical_not(polar))
        def _():
            attend(g, near)

        return carry

    lax.fori_loop(0, groups, step, 0)

    def drain(g, carry):
        for kind in range(3):
            own_copy(kind, g).wait_send()
        relay_copy(g).wait_send()
        return carry

    lax.fori_loop(0, groups, drain, 0)

    @pl.when(polar)
    def _():
        def drain_band(s, c):
            band_copy(s).wait_send()
            return c

        lax.fori_loop(1, n, drain_band, 0)


def local(n, n_lat, queries, key_tokens, value_tokens, block_lists, band_rows):
    tile_lat, tile_lon, feature = queries.shape
    tile = tile_lat * tile_lon
    picks = band_rows.shape[1]
    groups = feature // PAIR
    full = 5 * tile + n * picks
    vmem = pl.BlockSpec(memory_space=pltpu.VMEM)
    smem = pl.BlockSpec(memory_space=pltpu.SMEM)
    out = pl.pallas_call(
        functools.partial(kernel, n, n_lat, tile, picks),
        out_shape=jax.ShapeDtypeStruct((tile, feature), queries.dtype),
        in_specs=[vmem, vmem, vmem, smem, smem],
        out_specs=vmem,
        scratch_shapes=[
            pltpu.VMEM((groups, 2, full, PAIR), jnp.bfloat16),
            pltpu.VMEM((groups, 2, picks, PAIR), jnp.bfloat16),
            pltpu.VMEM((2, full), jnp.float32),
            pltpu.SemaphoreType.DMA((4, groups)),
            pltpu.SemaphoreType.DMA((4, groups)),
            pltpu.SemaphoreType.DMA((n,)),
            pltpu.SemaphoreType.DMA((n,)),
        ],
        compiler_params=pltpu.CompilerParams(
            collective_id=0, has_side_effects=True, vmem_limit_bytes=56 * 1024 * 1024
        ),
    )(
        queries.reshape(tile, feature),
        key_tokens.reshape(tile, feature),
        value_tokens.reshape(tile, feature),
        block_lists,
        band_rows,
    )
    return out.reshape(tile_lat, tile_lon, feature)


def solution(mesh):
    return jax.shard_map(
        functools.partial(local, mesh.shape["lon"], mesh.shape["lat"]),
        mesh=mesh,
        in_specs=(
            P("lat", "lon", None),
            P("lat", "lon", None),
            P("lat", "lon", None),
            P("lat", "lon", None),
            P("lat", "lon"),
        ),
        out_specs=P("lat", "lon", None),
        check_vma=False,
    )
```

time: 262 us -> 94 us (0.36)
  the two profiles are of different devices: /device:TPU:0 before, /device:TPU:8 now
where the time goes in v1:
time: 94 us; the launch traced here: 93.8 us
  Pallas kernels  91.7 us (98%)
  local copies, waits for them, and re-layouts  2.06 us (2%)
    pallas_call x1, Pallas kernels, local(): pl.pallas_call(functools.partial(kernel, n, n_lat, tile, picks), out_shap...  91.7 us
    unnamed x1, local copies, waits for them, and re-layouts  2.06 us

profile of v1, /device:TPU:8, one launch (start us, length us, event | category | flops | bytes accessed | tf_op | source)
XLA Modules:
  0.0 93.8 jit_solution(15303447264670435571)
XLA Ops:
  0.0 91.7 %shard_map.55 = bf16[256,1536]{1,0:T(8,128)(2,1)} custom-call(bf16[256,1536]{1,0:T(8,128)(2,1)} %bitcast.5, bf16[256,1536]{1,0:T(8,128)(2,1)} %bitcast.6, bf16[256,1536]{1,0:T(8,128)(2,1)} %bitcast.7, s32[2,1,8]{2,1,0:T(1,128)} %lists_ref.1, s32[1,16]{1,0:T(1,128)} %rows_ref.1), custom_call_target="tpu_custom_call" | custom-call | tf_op jit(solution)/shard_map/pallas_call | solution.py:230
  91.8 2.1 %copy.7 = bf16[16,16,1536]{2,1,0:T(8,128)(2,1)} copy(bf16[16,16,1536]{2,1,0:T(8,128)(2,1)} %bitcast.4) | data formatting | bytes 1572864

commit v2 on v1

--- a/solution.py
+++ b/solution.py
@@ -19,12 +19,14 @@
     n, n_lat, tile, picks,
     q_ref, k_ref, v_ref, lists_ref, rows_ref,
     out_ref,
-    kv, staged, bias, send_sem, recv_sem, band_send, band_recv,
+    kv, staged, selectors, bias, send_sem, recv_sem, far_send, far_recv, hot_send, hot_recv,
+    half_send, half_recv,
 ):
     groups = kv.shape[0]
     near = 5 * tile
     full = near + n * picks
     block = tile // 2
+    half = n // 2
     me = lax.axis_index("lon")
     lat = lax.axis_index("lat")
     polar = (lat == 0) | (lat == n_lat - 1)
@@ -35,18 +37,29 @@
 
     barrier = pltpu.get_barrier_semaphore()
 
-    def greet(step, carry):
-        pl.semaphore_signal(
-            barrier, inc=1, device_id={"lon": lax.rem(me + step, n)}, device_id_type=MESH
-        )
-        return carry
-
-    lax.fori_loop(1, n, greet, 0)
+    def greet(peer):
+        pl.semaphore_signal(barrier, inc=1, device_id={"lon": peer}, device_id_type=MESH)
+
+    greet(partner)
+    greet(east)
+    greet(west)
+
+    @pl.when(polar)
+    def _():
+        def greet_far(step, carry):
+            greet(lax.rem(me + 2 * step, n))
+            return carry
+
+        lax.fori_loop(2, half - 1, greet_far, 0)
 
     for g in range(groups):
         columns = slice(g * PAIR, (g + 1) * PAIR)
         kv[g, 0, 2 * tile:3 * tile, :] = k_ref[:, columns]
         kv[g, 1, 2 * tile:3 * tile, :] = v_ref[:, columns]
+
+    def band_rows_of(j):
+        place = lax.rem(j, 2) * half + j // 2
+        return pl.ds(pl.multiple_of(near + place * picks, picks), picks)
 
     candidate = lax.broadcasted_iota(jnp.int32, (1, full), 1) // block
     for b in range(2):
@@ -63,12 +76,15 @@
         for i in range(picks):
             hot = jnp.where((row == i) & (token == rows_ref[0, i]), 1.0, hot)
         hot = hot.astype(jnp.bfloat16)
+        selectors[1] = hot
         for which, ref in enumerate((k_ref, v_ref)):
             picked = jnp.dot(hot, ref[...], preferred_element_type=jnp.float32).astype(jnp.bfloat16)
             for g in range(groups):
-                staged[g, which] = picked[:, g * PAIR:(g + 1) * PAIR]
-
-    pl.semaphore_wait(barrier, n - 1)
+                chunk = picked[:, g * PAIR:(g + 1) * PAIR]
+                staged[g, which] = chunk
+                kv[g, which, band_rows_of(me), :] = chunk
+
+    pl.semaphore_wait(barrier, jnp.where(polar, half, 3))
 
     def tile_rows(t):
         return pl.ds(pl.multiple_of(t * tile, tile), tile)
@@ -94,26 +110,46 @@
             device_id_type=MESH,
         )
 
-    def band_rows_of(j):
-        return pl.ds(pl.multiple_of(near + j * picks, picks), picks)
-
-    def band_copy(step):
+    def far_copy(step):
         return pltpu.make_async_remote_copy(
             src_ref=staged,
             dst_ref=kv.at[:, :, band_rows_of(me)],
-            send_sem=band_send.at[step],
-            recv_sem=band_recv.at[step],
-            device_id={"lon": lax.rem(me + step, n)},
-            device_id_type=MESH,
-        )
-
-    def band_arrival(step):
+            send_sem=far_send.at[step],
+            recv_sem=far_recv.at[step],
+            device_id={"lon": lax.rem(me + 2 * step, n)},
+            device_id_type=MESH,
+        )
+
+    def far_arrival(step):
         return pltpu.make_async_remote_copy(
             src_ref=staged,
-            dst_ref=kv.at[:, :, band_rows_of(lax.rem(me + n - step, n))],
-            send_sem=band_send.at[step],
-            recv_sem=band_recv.at[step],
-            device_id={"lon": lax.rem(me + step, n)},
+            dst_ref=kv.at[:, :, band_rows_of(lax.rem(me + n - 2 * step, n))],
+            send_sem=far_send.at[step],
+            recv_sem=far_recv.at[step],
+            device_id={"lon": lax.rem(me + 2 * step, n)},
+            device_id_type=MESH,
+        )
+
+    def hot_copy(way):
+        return pltpu.make_async_remote_copy(
+            src_ref=selectors.at[1],
+            dst_ref=selectors.at[2 * way],
+            send_sem=hot_send.at[way],
+            recv_sem=hot_recv.at[way],
+            device_id={"lon": (east, west)[way]},
+            device_id_type=MESH,
+        )
+
+    def half_rows(parity):
+        return pl.ds(pl.multiple_of(near + parity * (half * picks), half * picks), half * picks)
+
+    def half_copy(g, parity):
+        return pltpu.make_async_remote_copy(
+            src_ref=kv.at[g, :, half_rows(parity)],
+            dst_ref=kv.at[g, :, half_rows(parity)],
+            send_sem=half_send.at[g],
+            recv_sem=half_recv.at[g],
+            device_id={"lon": partner},
             device_id_type=MESH,
         )
 
@@ -129,13 +165,14 @@
 
     @pl.when(polar)
     def _():
+        hot_copy(0).start()
+        hot_copy(1).start()
+
         def send(step, carry):
-            band_copy(step).start()
+            far_copy(step).start()
             return carry
 
-        lax.fori_loop(1, n, send, 0)
-        for g in range(groups):
-            kv[g, :, band_rows_of(me), :] = staged[g]
+        lax.fori_loop(2, half - 1, send, 0)
 
     def send_own(g, carry):
         for kind in range(3):
@@ -147,6 +184,16 @@
     def relay(g):
         arrival(1 - odd, 4 - 4 * odd, g).wait_recv()
         relay_copy(g).start()
+        arrival(odd, 4 * odd, g).wait_recv()
+
+        @pl.when(polar)
+        def _():
+            for which in range(2):
+                for way, peer in ((0, west), (2, east)):
+                    rows = kv[g, which, 2 * way * tile:(2 * way + 1) * tile, :]
+                    picked = jnp.dot(selectors[way], rows, preferred_element_type=jnp.float32)
+                    kv[g, which, band_rows_of(peer), :] = picked.astype(jnp.bfloat16)
+            half_copy(g, odd).start()
 
     def attend(g, rows):
         columns = pl.ds(pl.multiple_of(g * PAIR, PAIR), PAIR)
@@ -171,6 +218,17 @@
             results.append(mixed[:, :PAIR] / mixed[:, PAIR:])
         out_ref[:, columns] = jnp.where(first, results[0], results[1]).astype(out_ref.dtype)
 
+    @pl.when(polar)
+    def _():
+        hot_copy(0).wait_recv()
+        hot_copy(1).wait_recv()
+
+        def take(s, c):
+            far_arrival(s).wait_recv()
+            return c
+
+        lax.fori_loop(2, half - 1, take, 0)
+
     relay(0)
 
     def step(g, carry):
@@ -178,20 +236,12 @@
         def _():
             relay(g + 1)
 
-        arrival(odd, 4 * odd, g).wait_recv()
         arrival(2, 3 - 2 * odd, g).wait_recv()
         arrival(3, 1 + 2 * odd, g).wait_recv()
 
         @pl.when(polar)
         def _():
-            @pl.when(g == 0)
-            def _():
-                def take(s, c):
-                    band_arrival(s).wait_recv()
-                    return c
-
-                lax.fori_loop(1, n, take, 0)
-
+            half_copy(g, 1 - odd).wait_recv()
             attend(g, full)
 
         @pl.when(jnp.logical_not(polar))
@@ -212,11 +262,20 @@
 
     @pl.when(polar)
     def _():
-        def drain_band(s, c):
-            band_copy(s).wait_send()
+        hot_copy(0).wait_send()
+        hot_copy(1).wait_send()
+
+        def drain_far(s, c):
+            far_copy(s).wait_send()
             return c
 
-        lax.fori_loop(1, n, drain_band, 0)
+        lax.fori_loop(2, half - 1, drain_far, 0)
+
+        def drain_half(g, c):
+            half_copy(g, odd).wait_send()
+            return c
+
+        lax.fori_loop(0, groups, drain_half, 0)
 
 
 def local(n, n_lat, queries, key_tokens, value_tokens, block_lists, band_rows):
@@ -235,14 +294,19 @@
         scratch_shapes=[
             pltpu.VMEM((groups, 2, full, PAIR), jnp.bfloat16),
             pltpu.VMEM((groups, 2, picks, PAIR), jnp.bfloat16),
+            pltpu.VMEM((3, picks, tile), jnp.bfloat16),
             pltpu.VMEM((2, full), jnp.float32),
             pltpu.SemaphoreType.DMA((4, groups)),
             pltpu.SemaphoreType.DMA((4, groups)),
-            pltpu.SemaphoreType.DMA((n,)),
-            pltpu.SemaphoreType.DMA((n,)),
+            pltpu.SemaphoreType.DMA((n // 2,)),
+            pltpu.SemaphoreType.DMA((n // 2,)),
+            pltpu.SemaphoreType.DMA((2,)),
+            pltpu.SemaphoreType.DMA((2,)),
+            pltpu.SemaphoreType.DMA((groups,)),
+            pltpu.SemaphoreType.DMA((groups,)),
         ],
         compiler_params=pltpu.CompilerParams(
-            collective_id=0, has_side_effects=True, vmem_limit_bytes=56 * 1024 * 1024
+            collective_id=0, has_side_effects=True, vmem_limit_bytes=36 * 1024 * 1024
         ),
     )(
         queries.reshape(tile, feature),

time: 94 us -> 89.4 us (0.951)
  the two profiles are of different devices: /device:TPU:8 before, /device:TPU:0 now
where the time goes in v2:
time: 89.4 us; the launch traced here: 89.1 us
  Pallas kernels  84.1 us (94%)
  local copies, waits for them, and re-layouts  4.96 us (6%)
    pallas_call x1, Pallas kernels, local(): pl.pallas_call(functools.partial(kernel, n, n_lat, tile, picks), out_shap...  84.1 us
    unnamed x11, local copies, waits for them, and re-layouts  4.96 us

profile of v2, /device:TPU:0, one launch (start us, length us, event | category | flops | bytes accessed | tf_op | source)
XLA Modules:
  0.0 89.1 jit_solution(15830926384587628136)
XLA Ops:
  0.0 0.0 copy-start.3
  0.0 0.0 copy-start.4
  0.0 0.7 copy-done.3
  0.7 0.0 copy-done.4
  0.7 0.0 copy-start
  0.7 1.1 %copy-done = bf16[16,16,1536]{2,1,0:T(8,128)(2,1)S(1)} copy-done((bf16[16,16,1536]{2,1,0:T(8,128)(2,1)S(1)}, bf16[16,16,1536]{2,1,0:T(8,128)(2,1)}, u32[]{:S(2)}) %copy-start) | copy-done | bytes 786456
  1.8 0.0 copy-start.1
  1.8 1.1 %copy-done.1 = bf16[16,16,1536]{2,1,0:T(8,128)(2,1)S(1)} copy-done((bf16[16,16,1536]{2,1,0:T(8,128)(2,1)S(1)}, bf16[16,16,1536]{2,1,0:T(8,128)(2,1)}, u32[]{:S(2)}) %copy-start.1) | copy-done | bytes 786456
  3.0 0.0 copy-start.2
  3.0 1.1 %copy-done.2 = bf16[16,16,1536]{2,1,0:T(8,128)(2,1)S(1)} copy-done((bf16[16,16,1536]{2,1,0:T(8,128)(2,1)S(1)}, bf16[16,16,1536]{2,1,0:T(8,128)(2,1)}, u32[]{:S(2)}) %copy-start.2) | copy-done | bytes 786456
  4.1 84.1 %shard_map.55 = bf16[256,1536]{1,0:T(8,128)(2,1)S(1)} custom-call(bf16[256,1536]{1,0:T(8,128)(2,1)S(1)} %bitcast.5, bf16[256,1536]{1,0:T(8,128)(2,1)S(1)} %bitcast.6, bf16[256,1536]{1,0:T(8,128)(2,1)S(1)} %bitcast.7, s32[2,1,8]{2,1,0:T(1,128)S(1)} %copy-done.3, s32[1,16]{1,0:T(1,128)S(1)} %copy-done.4), custom_call_target="tpu_custom_call" | custom-call | tf_op jit(solution)/shard_map/pallas_call | solution.py:289
  88.2 0.9 copy.7
Async XLA Ops:
  0.0 0.7 copy-start.3
  0.0 0.7 copy-start.4
  0.7 1.1 %copy-start = (bf16[16,16,1536]{2,1,0:T(8,128)(2,1)S(1)}, bf16[16,16,1536]{2,1,0:T(8,128)(2,1)}, u32[]{:S(2)}) copy-start(bf16[16,16,1536]{2,1,0:T(8,128)(2,1)} %param.5) | copy-start | bytes 2359300
  1.8 1.1 %copy-start.1 = (bf16[16,16,1536]{2,1,0:T(8,128)(2,1)S(1)}, bf16[16,16,1536]{2,1,0:T(8,128)(2,1)}, u32[]{:S(2)}) copy-start(bf16[16,16,1536]{2,1,0:T(8,128)(2,1)} %param.6) | copy-start | bytes 2359300
  3.0 1.1 %copy-start.2 = (bf16[16,16,1536]{2,1,0:T(8,128)(2,1)S(1)}, bf16[16,16,1536]{2,1,0:T(8,128)(2,1)}, u32[]{:S(2)}) copy-start(bf16[16,16,1536]{2,1,0:T(8,128)(2,1)} %param.7) | copy-start | bytes 2359300

commit v3 on v2

v3 whole, which is shorter than its diff:
```python
import functools

import jax
import jax.numpy as jnp
from jax import lax
from jax.experimental import pallas as pl
from jax.experimental.pallas import tpu as pltpu
from jax.sharding import PartitionSpec as P

HD = 64
BR = 8
BW = 16
PAIR = 2 * HD
MASKED = -1e30
MESH = pl.DeviceIdType.MESH


def kernel(
    n, n_lat, tile, picks,
    q_in, k_in, v_in, lists_ref, rows_ref,
    out_ref,
    q_ref, kv, staged, selectors, bias, send_sem, recv_sem, far_send, far_recv, hot_send, hot_recv,
    half_send, half_recv, load_sem, q_sem,
):
    groups = kv.shape[0]
    near = 5 * tile
    full = near + n * picks
    block = tile // 2
    half = n // 2
    early = 2
    me = lax.axis_index("lon")
    lat = lax.axis_index("lat")
    polar = (lat == 0) | (lat == n_lat - 1)
    odd = lax.rem(me, 2)
    partner = me + 1 - 2 * odd
    east = lax.rem(me + 2, n)
    west = lax.rem(me + n - 2, n)

    def load(g, which):
        columns = pl.ds(pl.multiple_of(g * PAIR, PAIR), PAIR)
        return pltpu.make_async_copy(
            (k_in, v_in)[which].at[:, columns],
            kv.at[g, which, pl.ds(2 * tile, tile)],
            load_sem.at[which, g],
        )

    for g in range(groups):
        load(g, 0).start()
        load(g, 1).start()
    q_load = pltpu.make_async_copy(q_in, q_ref, q_sem)
    q_load.start()

    barrier = pltpu.get_barrier_semaphore()

    def greet(peer):
        pl.semaphore_signal(barrier, inc=1, device_id={"lon": peer}, device_id_type=MESH)

    greet(partner)
    greet(east)
    greet(west)

    @pl.when(polar)
    def _():
        def greet_far(step, carry):
            greet(lax.rem(me + 2 * step, n))
            return carry

        lax.fori_loop(2, half - 1, greet_far, 0)

    def band_rows_of(j):
        place = lax.rem(j, 2) * half + j // 2
        return pl.ds(pl.multiple_of(near + place * picks, picks), picks)

    pl.semaphore_wait(barrier, jnp.where(polar, half, 3))

    def tile_rows(t):
        return pl.ds(pl.multiple_of(t * tile, tile), tile)

    def own_copy(kind, g):
        target, t = ((east, 0), (west, 4), (partner, 1 + 2 * odd))[kind]
        return pltpu.make_async_remote_copy(
            src_ref=kv.at[g, :, tile_rows(2)],
            dst_ref=kv.at[g, :, tile_rows(t)],
            send_sem=send_sem.at[kind, g],
            recv_sem=recv_sem.at[kind, g],
            device_id={"lon": target},
            device_id_type=MESH,
        )

    def relay_copy(g):
        return pltpu.make_async_remote_copy(
            src_ref=kv.at[g, :, tile_rows(4 - 4 * odd)],
            dst_ref=kv.at[g, :, tile_rows(3 - 2 * odd)],
            send_sem=send_sem.at[3, g],
            recv_sem=recv_sem.at[3, g],
            device_id={"lon": partner},
            device_id_type=MESH,
        )

    def far_copy(step):
        return pltpu.make_async_remote_copy(
            src_ref=staged,
            dst_ref=kv.at[:, :, band_rows_of(me)],
            send_sem=far_send.at[step],
            recv_sem=far_recv.at[step],
            device_id={"lon": lax.rem(me + 2 * step, n)},
            device_id_type=MESH,
        )

    def far_arrival(step):
        return pltpu.make_async_remote_copy(
            src_ref=staged,
            dst_ref=kv.at[:, :, band_rows_of(lax.rem(me + n - 2 * step, n))],
            send_sem=far_send.at[step],
            recv_sem=far_recv.at[step],
            device_id={"lon": lax.rem(me + 2 * step, n)},
            device_id_type=MESH,
        )

    def hot_copy(way):
        return pltpu.make_async_remote_copy(
            src_ref=selectors.at[1],
            dst_ref=selectors.at[2 * way],
            send_sem=hot_send.at[way],
            recv_sem=hot_recv.at[way],
            device_id={"lon": (east, west)[way]},
            device_id_type=MESH,
        )

    def half_rows(parity):
        return pl.ds(pl.multiple_of(near + parity * (half * picks), half * picks), half * picks)

    def half_copy(g, parity):
        return pltpu.make_async_remote_copy(
            src_ref=kv.at[g, :, half_rows(parity)],
            dst_ref=kv.at[g, :, half_rows(parity)],
            send_sem=half_send.at[g],
            recv_sem=half_recv.at[g],
            device_id={"lon": partner},
            device_id_type=MESH,
        )

    def arrival(kind, t, g):
        return pltpu.make_async_remote_copy(
            src_ref=kv.at[g, :, tile_rows(2)],
            dst_ref=kv.at[g, :, tile_rows(t)],
            send_sem=send_sem.at[0, g],
            recv_sem=recv_sem.at[kind, g],
            device_id={"lon": partner},
            device_id_type=MESH,
        )

    def send_own(g, carry):
        load(g, 0).wait()
        load(g, 1).wait()
        for kind in range(3):
            own_copy(kind, g).start()
        return carry

    lax.fori_loop(0, early, send_own, 0)

    @pl.when(polar)
    def _():
        row = lax.broadcasted_iota(jnp.int32, (picks, tile), 0)
        token = lax.broadcasted_iota(jnp.int32, (picks, tile), 1)
        hot = jnp.zeros((picks, tile), jnp.float32)
        for i in range(picks):
            hot = jnp.where((row == i) & (token == rows_ref[0, i]), 1.0, hot)
        selectors[1] = hot.astype(jnp.bfloat16)
        hot_copy(0).start()
        hot_copy(1).start()

    def await_load(g, carry):
        load(g, 0).wait()
        load(g, 1).wait()
        return carry

    lax.fori_loop(early, groups, await_load, 0)

    @pl.when(polar)
    def _():
        def pick_own(g, carry):
            for which in range(2):
                rows = kv[g, which, 2 * tile:3 * tile, :]
                picked = jnp.dot(selectors[1], rows, preferred_element_type=jnp.float32)
                staged[g, which] = picked.astype(jnp.bfloat16)
                kv[g, which, band_rows_of(me), :] = picked.astype(jnp.bfloat16)
            return carry

        lax.fori_loop(0, groups, pick_own, 0)

        def send(step, carry):
            far_copy(step).start()
            return carry

        lax.fori_loop(2, half - 1, send, 0)

    def send_rest(g, carry):
        for kind in range(3):
            own_copy(kind, g).start()
        return carry

    lax.fori_loop(early, groups, send_rest, 0)

    candidate = lax.broadcasted_iota(jnp.int32, (1, full), 1) // block
    for b in range(2):
        listed = candidate >= 10
        for slot in range(lists_ref.shape[2]):
            listed = listed | (candidate == lists_ref[b, 0, slot])
        bias[b:b + 1, :] = jnp.where(listed, 0.0, MASKED)

    q_load.wait()

    def relay(g):
        arrival(1 - odd, 4 - 4 * odd, g).wait_recv()
        relay_copy(g).start()
        arrival(odd, 4 * odd, g).wait_recv()

        @pl.when(polar)
        def _():
            for which in range(2):
                for way, peer in ((0, west), (2, east)):
                    rows = kv[g, which, 2 * way * tile:(2 * way + 1) * tile, :]
                    picked = jnp.dot(selectors[way], rows, preferred_element_type=jnp.float32)
                    kv[g, which, band_rows_of(peer), :] = picked.astype(jnp.bfloat16)
            half_copy(g, odd).start()

    def attend(g, rows):
        columns = pl.ds(pl.multiple_of(g * PAIR, PAIR), PAIR)
        q = q_ref[:, columns] * jnp.bfloat16(HD ** -0.5)
        keys = kv[g, 0, 0:rows, :]
        values = jnp.concatenate(
            [kv[g, 1, 0:rows, :], jnp.ones((rows, PAIR), jnp.bfloat16)], axis=1
        )
        first = lax.broadcasted_iota(jnp.int32, (tile, PAIR), 1) < HD
        results = []
        for head in range(2):
            mine = first if head == 0 else ~first
            q_head = jnp.where(mine, q, jnp.zeros_like(q))
            scores = lax.dot_general(
                q_head, keys, (((1,), (1,)), ((), ())), preferred_element_type=jnp.float32
            )
            scores = scores.reshape(2, block, rows) + bias[:, 0:rows][:, None, :]
            scores = scores.reshape(tile, rows)
            row_max = jnp.max(scores, axis=-1, keepdims=True)
            weights = jnp.exp(scores - row_max).astype(jnp.bfloat16)
            mixed = jnp.dot(weights, values, preferred_element_type=jnp.float32)
            results.append(mixed[:, :PAIR] / mixed[:, PAIR:])
        out_ref[:, columns] = jnp.where(first, results[0], results[1]).astype(out_ref.dtype)

    @pl.when(polar)
    def _():
        hot_copy(0).wait_recv()
        hot_copy(1).wait_recv()

        def take(s, c):
            far_arrival(s).wait_recv()
            return c

        lax.fori_loop(2, half - 1, take, 0)

    relay(0)

    def step(g, carry):
        @pl.when(g + 1 < groups)
        def _():
            relay(g + 1)

        arrival(2, 3 - 2 * odd, g).wait_recv()
        arrival(3, 1 + 2 * odd, g).wait_recv()

        @pl.when(polar)
        def _():
            half_copy(g, 1 - odd).wait_recv()
            attend(g, full)

        @pl.when(jnp.logical_not(polar))
        def _():
            attend(g, near)

        return carry

    lax.fori_loop(0, groups, step, 0)

    def drain(g, carry):
        for kind in range(3):
            own_copy(kind, g).wait_send()
        relay_copy(g).wait_send()
        return carry

    lax.fori_loop(0, groups, drain, 0)

    @pl.when(polar)
    def _():
        hot_copy(0).wait_send()
        hot_copy(1).wait_send()

        def drain_far(s, c):
            far_copy(s).wait_send()
            return c

        lax.fori_loop(2, half - 1, drain_far, 0)

        def drain_half(g, c):
            half_copy(g, odd).wait_send()
            return c

        lax.fori_loop(0, groups, drain_half, 0)


def local(n, n_lat, queries, key_tokens, value_tokens, block_lists, band_rows):
    tile_lat, tile_lon, feature = queries.shape
    tile = tile_lat * tile_lon
    picks = band_rows.shape[1]
    groups = feature // PAIR
    full = 5 * tile + n * picks
    vmem = pl.BlockSpec(memory_space=pltpu.VMEM)
    hbm = pl.BlockSpec(memory_space=pltpu.HBM)
    smem = pl.BlockSpec(memory_space=pltpu.SMEM)
    out = pl.pallas_call(
        functools.partial(kernel, n, n_lat, tile, picks),
        out_shape=jax.ShapeDtypeStruct((tile, feature), queries.dtype),
        in_specs=[hbm, hbm, hbm, smem, smem],
        out_specs=vmem,
        scratch_shapes=[
            pltpu.VMEM((tile, feature), queries.dtype),
            pltpu.VMEM((groups, 2, full, PAIR), jnp.bfloat16),
            pltpu.VMEM((groups, 2, picks, PAIR), jnp.bfloat16),
            pltpu.VMEM((3, picks, tile), jnp.bfloat16),
            pltpu.VMEM((2, full), jnp.float32),
            pltpu.SemaphoreType.DMA((4, groups)),
            pltpu.SemaphoreType.DMA((4, groups)),
            pltpu.SemaphoreType.DMA((n // 2,)),
            pltpu.SemaphoreType.DMA((n // 2,)),
            pltpu.SemaphoreType.DMA((2,)),
            pltpu.SemaphoreType.DMA((2,)),
            pltpu.SemaphoreType.DMA((groups,)),
            pltpu.SemaphoreType.DMA((groups,)),
            pltpu.SemaphoreType.DMA((2, groups)),
            pltpu.SemaphoreType.DMA,
        ],
        compiler_params=pltpu.CompilerParams(
            collective_id=0, has_side_effects=True, vmem_limit_bytes=56 * 1024 * 1024
        ),
    )(
        queries.reshape(tile, feature),
        key_tokens.reshape(tile, feature),
        value_tokens.reshape(tile, feature),
        block_lists,
        band_rows,
    )
    return out.reshape(tile_lat, tile_lon, feature)


def solution(mesh):
    return jax.shard_map(
        functools.partial(local, mesh.shape["lon"], mesh.shape["lat"]),
        mesh=mesh,
        in_specs=(
            P("lat", "lon", None),
            P("lat", "lon", None),
            P("lat", "lon", None),
            P("lat", "lon", None),
            P("lat", "lon"),
        ),
        out_specs=P("lat", "lon", None),
        check_vma=False,
    )
```

time: 89.4 us -> 87.6 us (0.980)
  local copies, waits for them, and re-layouts: 4.96 us -> 2.06 us
  Pallas kernels: 84.1 us -> 85.4 us
    unnamed x11 -> x1, local copies, waits for them, and re-layouts: 4.96 us -> 2.06 us
    pallas_call x1, Pallas kernels: 84.1 us -> 85.4 us  [local(): pl.pallas_call(functools.partial(kernel, n, n_lat, tile, picks), out_shap...]
where the time goes in v3:
time: 87.6 us; the launch traced here: 87.5 us
  Pallas kernels  85.4 us (97%)
  local copies, waits for them, and re-layouts  2.06 us (2%)
    pallas_call x1, Pallas kernels, local(): pl.pallas_call(functools.partial(kernel, n, n_lat, tile, picks), out_shap...  85.4 us
    unnamed x1, local copies, waits for them, and re-layouts  2.06 us

profile of v3, /device:TPU:0, one launch (start us, length us, event | category | flops | bytes accessed | tf_op | source)
XLA Modules:
  0.0 87.5 jit_solution(2180291660432003176)
XLA Ops:
  0.0 85.4 %shard_map.55 = bf16[256,1536]{1,0:T(8,128)(2,1)} custom-call(bf16[256,1536]{1,0:T(8,128)(2,1)} %bitcast.5, bf16[256,1536]{1,0:T(8,128)(2,1)} %bitcast.6, bf16[256,1536]{1,0:T(8,128)(2,1)} %bitcast.7, s32[2,1,8]{2,1,0:T(1,128)} %lists_ref.1, s32[1,16]{1,0:T(1,128)} %rows_ref.1), custom_call_target="tpu_custom_call" | custom-call | tf_op jit(solution)/shard_map/pallas_call | solution.py:320
  85.4 2.1 %copy.7 = bf16[16,16,1536]{2,1,0:T(8,128)(2,1)} copy(bf16[16,16,1536]{2,1,0:T(8,128)(2,1)} %bitcast.4) | data formatting | bytes 1572864

commit v4 on v3

--- a/solution.py
+++ b/solution.py
@@ -28,6 +28,7 @@
     block = tile // 2
     half = n // 2
     early = 2
+    window = 4
     me = lax.axis_index("lon")
     lat = lax.axis_index("lat")
     polar = (lat == 0) | (lat == n_lat - 1)
@@ -200,7 +201,7 @@
             own_copy(kind, g).start()
         return carry
 
-    lax.fori_loop(early, groups, send_rest, 0)
+    lax.fori_loop(early, window, send_rest, 0)
 
     candidate = lax.broadcasted_iota(jnp.int32, (1, full), 1) // block
     for b in range(2):
@@ -266,6 +267,13 @@
         def _():
             relay(g + 1)
 
+        @pl.when(g + window < groups)
+        def _():
+            for kind in range(3):
+                own_copy(kind, g).wait_send()
+            for kind in range(3):
+                own_copy(kind, g + window).start()
+
         arrival(2, 3 - 2 * odd, g).wait_recv()
         arrival(3, 1 + 2 * odd, g).wait_recv()
 
@@ -283,8 +291,11 @@
     lax.fori_loop(0, groups, step, 0)
 
     def drain(g, carry):
-        for kind in range(3):
-            own_copy(kind, g).wait_send()
+        @pl.when(g + window >= groups)
+        def _():
+            for kind in range(3):
+                own_copy(kind, g).wait_send()
+
         relay_copy(g).wait_send()
         return carry
 
@@ -340,7 +351,7 @@
             pltpu.SemaphoreType.DMA,
         ],
         compiler_params=pltpu.CompilerParams(
-            collective_id=0, has_side_effects=True, vmem_limit_bytes=56 * 1024 * 1024
+            collective_id=0, has_side_effects=True, vmem_limit_bytes=53 * 1024 * 1024
         ),
     )(
         queries.reshape(tile, feature),

time: 87.6 us -> 86.5 us (0.987)
    unnamed x1 -> x5, local copies, waits for them, and re-layouts: 2.06 us -> 1.56 us
where the time goes in v4:
time: 86.5 us; the launch traced here: 86.3 us
  Pallas kernels  84.8 us (98%)
  local copies, waits for them, and re-layouts  1.56 us (2%)
    pallas_call x1, Pallas kernels, local(): pl.pallas_call(functools.partial(kernel, n, n_lat, tile, picks), out_shap...  84.8 us

profile of v4, /device:TPU:0, one launch (start us, length us, event | category | flops | bytes accessed | tf_op | source)
XLA Modules:
  0.0 86.3 jit_solution(16494726934643811452)
XLA Ops:
  0.0 0.0 copy-start
  0.0 0.0 copy-start.1
  0.0 0.7 copy-done
  0.7 0.0 copy-done.1
  0.7 84.8 %shard_map.55 = bf16[256,1536]{1,0:T(8,128)(2,1)S(1)} custom-call(bf16[256,1536]{1,0:T(8,128)(2,1)} %bitcast.5, bf16[256,1536]{1,0:T(8,128)(2,1)} %bitcast.6, bf16[256,1536]{1,0:T(8,128)(2,1)} %bitcast.7, s32[2,1,8]{2,1,0:T(1,128)S(1)} %copy-done, s32[1,16]{1,0:T(1,128)S(1)} %copy-done.1), custom_call_target="tpu_custom_call" | custom-call | tf_op jit(solution)/shard_map/pallas_call | solution.py:331
  85.5 0.9 %copy.7 = bf16[16,16,1536]{2,1,0:T(8,128)(2,1)} copy(bf16[16,16,1536]{2,1,0:T(8,128)(2,1)S(1)} %bitcast.4) | data formatting | bytes 1572864
Async XLA Ops:
  0.0 0.7 copy-start
  0.0 0.7 copy-start.1

commit v5 on v4

--- a/solution.py
+++ b/solution.py
@@ -20,7 +20,7 @@
     q_in, k_in, v_in, lists_ref, rows_ref,
     out_ref,
     q_ref, kv, staged, selectors, bias, send_sem, recv_sem, far_send, far_recv, hot_send, hot_recv,
-    half_send, half_recv, load_sem, q_sem,
+    outer_send, outer_recv, beyond_send, beyond_recv, load_sem, q_sem,
 ):
     groups = kv.shape[0]
     near = 5 * tile
@@ -45,29 +45,29 @@
             load_sem.at[which, g],
         )
 
+    barrier = pltpu.get_barrier_semaphore()
+
+    def greet(peer):
+        pl.semaphore_signal(barrier, inc=1, device_id={"lon": peer}, device_id_type=MESH)
+
+    greet(partner)
+    greet(east)
+    greet(west)
+
+    @pl.when(polar)
+    def _():
+        def greet_far(step, carry):
+            greet(lax.rem(me + 2 * step, n))
+            return carry
+
+        lax.fori_loop(2, half - 1, greet_far, 0)
+
     for g in range(groups):
         load(g, 0).start()
         load(g, 1).start()
     q_load = pltpu.make_async_copy(q_in, q_ref, q_sem)
     q_load.start()
 
-    barrier = pltpu.get_barrier_semaphore()
-
-    def greet(peer):
-        pl.semaphore_signal(barrier, inc=1, device_id={"lon": peer}, device_id_type=MESH)
-
-    greet(partner)
-    greet(east)
-    greet(west)
-
-    @pl.when(polar)
-    def _():
-        def greet_far(step, carry):
-            greet(lax.rem(me + 2 * step, n))
-            return carry
-
-        lax.fori_loop(2, half - 1, greet_far, 0)
-
     def band_rows_of(j):
         place = lax.rem(j, 2) * half + j // 2
         return pl.ds(pl.multiple_of(near + place * picks, picks), picks)
@@ -118,28 +118,57 @@
             device_id_type=MESH,
         )
 
-    def hot_copy(way):
-        return pltpu.make_async_remote_copy(
-            src_ref=selectors.at[1],
-            dst_ref=selectors.at[2 * way],
-            send_sem=hot_send.at[way],
-            recv_sem=hot_recv.at[way],
-            device_id={"lon": (east, west)[way]},
-            device_id_type=MESH,
-        )
-
-    def half_rows(parity):
-        return pl.ds(pl.multiple_of(near + parity * (half * picks), half * picks), half * picks)
-
-    def half_copy(g, parity):
-        return pltpu.make_async_remote_copy(
-            src_ref=kv.at[g, :, half_rows(parity)],
-            dst_ref=kv.at[g, :, half_rows(parity)],
-            send_sem=half_send.at[g],
-            recv_sem=half_recv.at[g],
+    def hot_copy(kind):
+        target, t = ((east, 0), (west, 4), (partner, 1 + 2 * odd), (partner, 3 - 2 * odd))[kind]
+        return pltpu.make_async_remote_copy(
+            src_ref=selectors.at[2 if kind < 3 else 4 - 4 * odd],
+            dst_ref=selectors.at[t],
+            send_sem=hot_send.at[kind],
+            recv_sem=hot_recv.at[kind],
+            device_id={"lon": target},
+            device_id_type=MESH,
+        )
+
+    def hot_arrival(kind):
+        t = (0, 4, 3 - 2 * odd, 1 + 2 * odd)[kind]
+        return pltpu.make_async_remote_copy(
+            src_ref=selectors.at[2],
+            dst_ref=selectors.at[t],
+            send_sem=hot_send.at[kind],
+            recv_sem=hot_recv.at[kind],
             device_id={"lon": partner},
             device_id_type=MESH,
         )
+
+    def outer_rows(j):
+        return band_rows_of(lax.rem(j + n + 4 * lax.rem(j, 2) - 2, n))
+
+    def outer_copy(g, j):
+        return pltpu.make_async_remote_copy(
+            src_ref=kv.at[g, :, outer_rows(j)],
+            dst_ref=kv.at[g, :, outer_rows(j)],
+            send_sem=outer_send.at[g],
+            recv_sem=outer_recv.at[g],
+            device_id={"lon": partner},
+            device_id_type=MESH,
+        )
+
+    def beyond_copy(step, j):
+        rows = band_rows_of(lax.rem(j + n - 2 * step, n))
+        return pltpu.make_async_remote_copy(
+            src_ref=kv.at[:, :, rows],
+            dst_ref=kv.at[:, :, rows],
+            send_sem=beyond_send.at[step],
+            recv_sem=beyond_recv.at[step],
+            device_id={"lon": partner},
+            device_id_type=MESH,
+        )
+
+    def pick(g, t, peer):
+        for which in range(2):
+            rows = kv[g, which, tile_rows(t), :]
+            picked = jnp.dot(selectors[t], rows, preferred_element_type=jnp.float32)
+            kv[g, which, band_rows_of(peer), :] = picked.astype(jnp.bfloat16)
 
     def arrival(kind, t, g):
         return pltpu.make_async_remote_copy(
@@ -167,9 +196,9 @@
         hot = jnp.zeros((picks, tile), jnp.float32)
         for i in range(picks):
             hot = jnp.where((row == i) & (token == rows_ref[0, i]), 1.0, hot)
-        selectors[1] = hot.astype(jnp.bfloat16)
-        hot_copy(0).start()
-        hot_copy(1).start()
+        selectors[2] = hot.astype(jnp.bfloat16)
+        for kind in range(3):
+            hot_copy(kind).start()
 
     def await_load(g, carry):
         load(g, 0).wait()
@@ -183,7 +212,7 @@
         def pick_own(g, carry):
             for which in range(2):
                 rows = kv[g, which, 2 * tile:3 * tile, :]
-                picked = jnp.dot(selectors[1], rows, preferred_element_type=jnp.float32)
+                picked = jnp.dot(selectors[2], rows, preferred_element_type=jnp.float32)
                 staged[g, which] = picked.astype(jnp.bfloat16)
                 kv[g, which, band_rows_of(me), :] = picked.astype(jnp.bfloat16)
             return carry
@@ -219,12 +248,9 @@
 
         @pl.when(polar)
         def _():
-            for which in range(2):
-                for way, peer in ((0, west), (2, east)):
-                    rows = kv[g, which, 2 * way * tile:(2 * way + 1) * tile, :]
-                    picked = jnp.dot(selectors[way], rows, preferred_element_type=jnp.float32)
-                    kv[g, which, band_rows_of(peer), :] = picked.astype(jnp.bfloat16)
-            half_copy(g, odd).start()
+            pick(g, 0, west)
+            pick(g, 4, east)
+            outer_copy(g, me).start()
 
     def attend(g, rows):
         columns = pl.ds(pl.multiple_of(g * PAIR, PAIR), PAIR)
@@ -251,11 +277,13 @@
 
     @pl.when(polar)
     def _():
-        hot_copy(0).wait_recv()
-        hot_copy(1).wait_recv()
+        for kind in range(2):
+            hot_arrival(kind).wait_recv()
+        hot_copy(3).start()
 
         def take(s, c):
             far_arrival(s).wait_recv()
+            beyond_copy(s, me).start()
             return c
 
         lax.fori_loop(2, half - 1, take, 0)
@@ -279,7 +307,20 @@
 
         @pl.when(polar)
         def _():
-            half_copy(g, 1 - odd).wait_recv()
+            @pl.when(g == 0)
+            def _():
+                hot_arrival(2).wait_recv()
+                hot_arrival(3).wait_recv()
+
+                def take_beyond(s, c):
+                    beyond_copy(s, partner).wait_recv()
+                    return c
+
+                lax.fori_loop(2, half - 1, take_beyond, 0)
+
+            pick(g, 3 - 2 * odd, partner)
+            pick(g, 1 + 2 * odd, lax.rem(me + n - 1 + 2 * odd, n))
+            outer_copy(g, partner).wait_recv()
             attend(g, full)
 
         @pl.when(jnp.logical_not(polar))
@@ -303,20 +344,21 @@
 
     @pl.when(polar)
     def _():
-        hot_copy(0).wait_send()
-        hot_copy(1).wait_send()
+        for kind in range(4):
+            hot_copy(kind).wait_send()
 
         def drain_far(s, c):
             far_copy(s).wait_send()
+            beyond_copy(s, me).wait_send()
             return c
 
         lax.fori_loop(2, half - 1, drain_far, 0)
 
-        def drain_half(g, c):
-            half_copy(g, odd).wait_send()
+        def drain_outer(g, c):
+            outer_copy(g, me).wait_send()
             return c
 
-        lax.fori_loop(0, groups, drain_half, 0)
+        lax.fori_loop(0, groups, drain_outer, 0)
 
 
 def local(n, n_lat, queries, key_tokens, value_tokens, block_lists, band_rows):
@@ -337,16 +379,18 @@
             pltpu.VMEM((tile, feature), queries.dtype),
             pltpu.VMEM((groups, 2, full, PAIR), jnp.bfloat16),
             pltpu.VMEM((groups, 2, picks, PAIR), jnp.bfloat16),
-            pltpu.VMEM((3, picks, tile), jnp.bfloat16),
+            pltpu.VMEM((5, picks, tile), jnp.bfloat16),
             pltpu.VMEM((2, full), jnp.float32),
             pltpu.SemaphoreType.DMA((4, groups)),
             pltpu.SemaphoreType.DMA((4, groups)),
             pltpu.SemaphoreType.DMA((n // 2,)),
             pltpu.SemaphoreType.DMA((n // 2,)),
-            pltpu.SemaphoreType.DMA((2,)),
-            pltpu.SemaphoreType.DMA((2,)),
+            pltpu.SemaphoreType.DMA((4,)),
+            pltpu.SemaphoreType.DMA((4,)),
             pltpu.SemaphoreType.DMA((groups,)),
             pltpu.SemaphoreType.DMA((groups,)),
+            pltpu.SemaphoreType.DMA((n // 2,)),
+            pltpu.SemaphoreType.DMA((n // 2,)),
             pltpu.SemaphoreType.DMA((2, groups)),
             pltpu.SemaphoreType.DMA,
         ],

time: 86.5 us -> 86 us (level)
  no operation moved by 1% of the time
where the time goes in v5:
time: 86 us; the launch traced here: 85.8 us
  Pallas kernels  84.3 us (98%)
  local copies, waits for them, and re-layouts  1.56 us (2%)
    pallas_call x1, Pallas kernels, local(): pl.pallas_call(functools.partial(kernel, n, n_lat, tile, picks), out_shap...  84.3 us

profile of v5, /device:TPU:0, one launch (start us, length us, event | category | flops | bytes accessed | tf_op | source)
XLA Modules:
  0.0 85.8 jit_solution(13445023034705365988)
XLA Ops:
  0.0 0.0 copy-start
  0.0 0.0 copy-start.1
  0.0 0.7 copy-done
  0.7 0.0 copy-done.1
  0.7 84.3 %shard_map.55 = bf16[256,1536]{1,0:T(8,128)(2,1)S(1)} custom-call(bf16[256,1536]{1,0:T(8,128)(2,1)} %bitcast.5, bf16[256,1536]{1,0:T(8,128)(2,1)} %bitcast.6, bf16[256,1536]{1,0:T(8,128)(2,1)} %bitcast.7, s32[2,1,8]{2,1,0:T(1,128)S(1)} %copy-done, s32[1,16]{1,0:T(1,128)S(1)} %copy-done.1), custom_call_target="tpu_custom_call" | custom-call | tf_op jit(solution)/shard_map/pallas_call | solution.py:373
  84.9 0.9 %copy.7 = bf16[16,16,1536]{2,1,0:T(8,128)(2,1)} copy(bf16[16,16,1536]{2,1,0:T(8,128)(2,1)S(1)} %bitcast.4) | data formatting | bytes 1572864
Async XLA Ops:
  0.0 0.7 copy-start
  0.0 0.7 copy-start.1

commit v6 on v5

--- a/solution.py
+++ b/solution.py
@@ -28,10 +28,10 @@
     block = tile // 2
     half = n // 2
     early = 2
-    window = 4
     me = lax.axis_index("lon")
     lat = lax.axis_index("lat")
     polar = (lat == 0) | (lat == n_lat - 1)
+    window = jnp.where(polar, 8, 2)
     odd = lax.rem(me, 2)
     partner = me + 1 - 2 * odd
     east = lax.rem(me + 2, n)

time: 86 us -> 97.5 us (1.13)
  the two profiles are of different devices: /device:TPU:0 before, /device:TPU:2 now
where the time goes in v6:
time: 97.5 us; the launch traced here: 97.4 us
  Pallas kernels  95.8 us (98%)
  local copies, waits for them, and re-layouts  1.56 us (2%)
    pallas_call x1, Pallas kernels, local(): pl.pallas_call(functools.partial(kernel, n, n_lat, tile, picks), out_shap...  95.8 us

profile of v6, /device:TPU:2, one launch (start us, length us, event | category | flops | bytes accessed | tf_op | source)
XLA Modules:
  0.0 97.4 jit_solution(3452275757503605140)
XLA Ops:
  0.0 0.0 copy-start
  0.0 0.0 copy-start.1
  0.0 0.7 copy-done
  0.7 0.0 copy-done.1
  0.7 95.8 %shard_map.55 = bf16[256,1536]{1,0:T(8,128)(2,1)S(1)} custom-call(bf16[256,1536]{1,0:T(8,128)(2,1)} %bitcast.5, bf16[256,1536]{1,0:T(8,128)(2,1)} %bitcast.6, bf16[256,1536]{1,0:T(8,128)(2,1)} %bitcast.7, s32[2,1,8]{2,1,0:T(1,128)S(1)} %copy-done, s32[1,16]{1,0:T(1,128)S(1)} %copy-done.1), custom_call_target="tpu_custom_call" | custom-call | tf_op jit(solution)/shard_map/pallas_call | solution.py:373
  96.5 0.9 copy.7
Async XLA Ops:
  0.0 0.7 copy-start
  0.0 0.7 copy-start.1

commit v7 on v6

--- a/solution.py
+++ b/solution.py
@@ -31,7 +31,7 @@
     me = lax.axis_index("lon")
     lat = lax.axis_index("lat")
     polar = (lat == 0) | (lat == n_lat - 1)
-    window = jnp.where(polar, 8, 2)
+    window = jnp.where(lat == 1, 3, 4)
     odd = lax.rem(me, 2)
     partner = me + 1 - 2 * odd
     east = lax.rem(me + 2, n)

time: 97.5 us -> 87.6 us (0.90)
  the two profiles are of different devices: /device:TPU:2 before, /device:TPU:0 now
where the time goes in v7:
time: 87.6 us; the launch traced here: 87.4 us
  Pallas kernels  85.8 us (98%)
  local copies, waits for them, and re-layouts  1.56 us (2%)
    pallas_call x1, Pallas kernels, local(): pl.pallas_call(functools.partial(kernel, n, n_lat, tile, picks), out_shap...  85.8 us

profile of v7, /device:TPU:0, one launch (start us, length us, event | category | flops | bytes accessed | tf_op | source)
XLA Modules:
  0.0 87.4 jit_solution(3696237621987571143)
XLA Ops:
  0.0 0.0 copy-start
  0.0 0.0 copy-start.1
  0.0 0.7 copy-done
  0.7 0.0 copy-done.1
  0.7 85.8 %shard_map.55 = bf16[256,1536]{1,0:T(8,128)(2,1)S(1)} custom-call(bf16[256,1536]{1,0:T(8,128)(2,1)} %bitcast.5, bf16[256,1536]{1,0:T(8,128)(2,1)} %bitcast.6, bf16[256,1536]{1,0:T(8,128)(2,1)} %bitcast.7, s32[2,1,8]{2,1,0:T(1,128)S(1)} %copy-done, s32[1,16]{1,0:T(1,128)S(1)} %copy-done.1), custom_call_target="tpu_custom_call" | custom-call | tf_op jit(solution)/shard_map/pallas_call | solution.py:373
  86.5 0.9 %copy.7 = bf16[16,16,1536]{2,1,0:T(8,128)(2,1)} copy(bf16[16,16,1536]{2,1,0:T(8,128)(2,1)S(1)} %bitcast.4) | data formatting | bytes 1572864
Async XLA Ops:
  0.0 0.7 copy-start
  0.0 0.7 copy-start.1

commit v8 on v7

--- a/solution.py
+++ b/solution.py
@@ -28,10 +28,10 @@
     block = tile // 2
     half = n // 2
     early = 2
+    window = 6
     me = lax.axis_index("lon")
     lat = lax.axis_index("lat")
     polar = (lat == 0) | (lat == n_lat - 1)
-    window = jnp.where(lat == 1, 3, 4)
     odd = lax.rem(me, 2)
     partner = me + 1 - 2 * odd
     east = lax.rem(me + 2, n)
@@ -244,10 +244,10 @@
     def relay(g):
         arrival(1 - odd, 4 - 4 * odd, g).wait_recv()
         relay_copy(g).start()
-        arrival(odd, 4 * odd, g).wait_recv()
 
         @pl.when(polar)
         def _():
+            arrival(odd, 4 * odd, g).wait_recv()
             pick(g, 0, west)
             pick(g, 4, east)
             outer_copy(g, me).start()
@@ -325,6 +325,7 @@
 
         @pl.when(jnp.logical_not(polar))
         def _():
+            arrival(odd, 4 * odd, g).wait_recv()
             attend(g, near)
 
         return carry

time: 87.6 us -> 86.4 us (0.986)
  Pallas kernels: 85.8 us -> 84.6 us
    pallas_call x1, Pallas kernels: 85.8 us -> 84.6 us  [local(): pl.pallas_call(functools.partial(kernel, n, n_lat, tile, picks), out_shap...]
where the time goes in v8:
time: 86.4 us; the launch traced here: 86.2 us
  Pallas kernels  84.6 us (98%)
  local copies, waits for them, and re-layouts  1.56 us (2%)
    pallas_call x1, Pallas kernels, local(): pl.pallas_call(functools.partial(kernel, n, n_lat, tile, picks), out_shap...  84.6 us

profile of v8, /device:TPU:0, one launch (start us, length us, event | category | flops | bytes accessed | tf_op | source)
XLA Modules:
  0.0 86.2 jit_solution(4398425338848467438)
XLA Ops:
  0.0 0.0 copy-start
  0.0 0.0 copy-start.1
  0.0 0.7 copy-done
  0.7 0.0 copy-done.1
  0.7 84.6 %shard_map.55 = bf16[256,1536]{1,0:T(8,128)(2,1)S(1)} custom-call(bf16[256,1536]{1,0:T(8,128)(2,1)} %bitcast.5, bf16[256,1536]{1,0:T(8,128)(2,1)} %bitcast.6, bf16[256,1536]{1,0:T(8,128)(2,1)} %bitcast.7, s32[2,1,8]{2,1,0:T(1,128)S(1)} %copy-done, s32[1,16]{1,0:T(1,128)S(1)} %copy-done.1), custom_call_target="tpu_custom_call" | custom-call | tf_op jit(solution)/shard_map/pallas_call | solution.py:374
  85.3 0.9 %copy.7 = bf16[16,16,1536]{2,1,0:T(8,128)(2,1)} copy(bf16[16,16,1536]{2,1,0:T(8,128)(2,1)S(1)} %bitcast.4) | data formatting | bytes 1572864
Async XLA Ops:
  0.0 0.7 copy-start
  0.0 0.7 copy-start.1
